TPU v7x, 32 devices: a whole 2x2x4 slice. The times are simulated.
32 devices in a mesh: groups: 2 (over y), vocab: 4 (over z), rows: 4 (over x, core).
Axes of the slice: x: 2, y: 2, z: 4, core: 2. Of those that a mesh axis runs over, the one named last changes fastest.
Arguments:
- llama_logits: bfloat16 [1024, 8192], P(('groups', 'rows'), 'vocab'), parts along dimension 0, may hold values from -64 to 620
- qwen_logits: bfloat16 [1024, 9728], P(('groups', 'rows'), 'vocab'), parts along dimension 0, may hold values from -64 to 620
- gemma_logits: bfloat16 [1024, 16384], P(('groups', 'rows'), 'vocab'), parts along dimension 0, may hold values from -64 to 620
- student_logits: bfloat16 [1024, 8192], P(('groups', 'rows'), 'vocab'), parts along dimension 0, may hold values from -64 to 620
- align_llama: int32 [128, 3], P('vocab'), may hold values from 0 to 63, as said below
- align_qwen: int32 [152, 3], P('vocab'), may hold values from 0 to 75, as said below
- align_gemma: int32 [256, 3], P('vocab'), may hold values from 0 to 127, as said below
- tiles: bfloat16 [16, 128, 128], replicated, as said below
- student_order: int32 [64], replicated, may hold values from 0 to 63, as said below
Outputs:
- row_loss: float32 [1024], P(('groups', 'rows')), parts along dimension 0
- grad: bfloat16 [1024, 8192], P(('groups', 'rows'), 'vocab'), parts along dimension 0
There are 2 independent parts, one for each index of `groups`. A program takes and returns all parts, laid end to end along the dimension named above; an argument that names none is the same for every part. Nothing has to cross between parts.
Inputs may be any that keep to these rules, and one draw needn't show every extreme that they name: `align_llama`: row e of block i of 32 rows names teacher block i * 16 + e // 2; column 1 is a student vocabulary block, column 2 a tile. Over the three lists, the rows of one block i name at most 4 different student blocks whose column block lies in any one range j * 16 to (j + 1) * 16 - 1 of position; for one range j this many from every block i. `align_qwen`: row e of block i of 38 rows names teacher block i * 19 + e // 2; columns as in align_llama, under the same bound. `align_gemma`: row e of block i of 64 rows names teacher block i * 32 + e // 2; columns as in align_llama, under the same bound. `student_order`: a permutation. `tiles`: nonnegative.
All inputs are finite; a program needn't handle non-finite values.
Results may differ from a plain program's by a relative error of at most 0.0041.
Values may be sent and summed in bfloat16 or wider, within the bound.
A program may use at most 128 MiB of HBM per device.

v0:
```python
import jax
import jax.numpy as jnp
from jax import lax
from jax.sharding import PartitionSpec as P

CAP = 4


TEMP = 2.0
SHARE = 1.0 / 3.0


def exp_total(scaled, highest):
    return jnp.sum(jnp.exp(scaled - highest[:, None]), axis=1)


def slot_sums(grids, picks, tile_sets, slot_lists, slots_total):
    result = None
    for grid, local_block, tile_rows, own_slots in zip(grids, picks, tile_sets, slot_lists):
        picked = jnp.take(grid, local_block, axis=1)
        mapped_part = (
            jnp.einsum("reb,ebc->erc", picked, tile_rows, preferred_element_type=jnp.float32)
            * SHARE
        )
        added = jax.ops.segment_sum(mapped_part, own_slots, num_segments=slots_total)
        result = added if result is None else result + added
    return result


def land(received, got_labels, span, row_count, block):
    slots_total = got_labels.size
    label_hot = (
        got_labels.reshape(-1)[:, None] == jnp.arange(span, dtype=jnp.int32)[None, :]
    ).astype(jnp.bfloat16)
    summed = jnp.dot(
        label_hot.T, received.reshape(slots_total, -1), preferred_element_type=jnp.float32
    )
    return jnp.transpose(summed.reshape(span, row_count, block), (1, 0, 2)).reshape(
        row_count, span * block
    )


def shards(
    llama_logits,
    qwen_logits,
    gemma_logits,
    student_logits,
    align_llama,
    align_qwen,
    align_gemma,
    tiles,
    student_order,
):
    vocab_index = lax.axis_index("vocab")
    owners = lax.axis_size("vocab")
    rows_here = student_logits.shape[0]
    block = tiles.shape[1]
    span = student_logits.shape[1] // block
    slots_total = owners * CAP
    teachers = (llama_logits, qwen_logits, gemma_logits)
    lists = (align_llama, align_qwen, align_gemma)
    scaled = [values.astype(jnp.float32) / TEMP for values in teachers]
    student_scaled = student_logits.astype(jnp.float32) / TEMP
    highest = [jnp.max(values, axis=1) for values in scaled]
    student_high = jnp.max(student_scaled, axis=1)
    teacher_peak = lax.pmax((highest[0], highest[1], highest[2]), "vocab")
    sum_llama = exp_total(scaled[0], teacher_peak[0])
    sum_qwen = exp_total(scaled[1], teacher_peak[1])
    sum_gemma = exp_total(scaled[2], teacher_peak[2])
    teacher_total = lax.psum((sum_llama, sum_qwen, sum_gemma), "vocab")
    student_peak = lax.pmax(student_high, "vocab")
    order_slots = (
        jnp.zeros((owners * span,), jnp.int32)
        .at[student_order]
        .set(jnp.arange(owners * span, dtype=jnp.int32))
    )
    column_all = order_slots[jnp.concatenate([align[:, 1] for align in lists])]
    present = jnp.zeros((owners * span,), jnp.int32).at[column_all].set(1)
    rank_table = (jnp.cumsum(present.reshape(owners, span), axis=1) - 1).reshape(-1)
    slot_all = column_all // span * CAP + rank_table[column_all]
    labels = jnp.full((slots_total,), span, jnp.int32).at[slot_all].set(column_all % span)
    label_grid = labels.reshape(owners, CAP)
    grids = []
    picks = []
    tile_sets = []
    slot_lists = []
    offset_all = 0
    for values, align, peak, total in zip(scaled, lists, teacher_peak, teacher_total):
        probs = (jnp.exp(values - peak[:, None]) / total[:, None]).astype(jnp.bfloat16)
        blocks_here = probs.shape[1] // block
        grids.append(probs.reshape(rows_here, blocks_here, block))
        picks.append(align[:, 0] - vocab_index * blocks_here)
        tile_sets.append(jnp.take(tiles, align[:, 2], axis=0))
        entry_count = align.shape[0]
        slot_lists.append(slot_all[offset_all : offset_all + entry_count])
        offset_all = offset_all + entry_count
    send_sum = slot_sums(grids, picks, tile_sets, slot_lists, slots_total)
    outgoing = send_sum.astype(jnp.bfloat16).reshape(owners, CAP, rows_here, block)
    received, got_labels = (
        lax.all_to_all(outgoing, "vocab", split_axis=0, concat_axis=0, tiled=True),
        lax.all_to_all(label_grid, "vocab", split_axis=0, concat_axis=0, tiled=True),
    )
    target = land(received, got_labels, span, rows_here, block)
    total_local = jnp.sum(target, axis=1)
    cross_local = jnp.sum(target * student_scaled, axis=1)
    student_local = exp_total(student_scaled, student_peak)
    row_total, cross, student_total = lax.psum((total_local, cross_local, student_local), "vocab")
    lse = student_peak + jnp.log(student_total)
    row_loss = row_total * lse - cross
    factor = owners * span * block / TEMP
    grad = (factor * (row_total[:, None] * jnp.exp(student_scaled - lse[:, None]) - target)).astype(
        jnp.bfloat16
    )
    return (row_loss, grad)


def solution(mesh):
    in_specs = (
        P(("groups", "rows"), "vocab"),
        P(("groups", "rows"), "vocab"),
        P(("groups", "rows"), "vocab"),
        P(("groups", "rows"), "vocab"),
        P("vocab", None),
        P("vocab", None),
        P("vocab", None),
        P(),
        P(),
    )
    out_specs = (P(("groups", "rows")), P(("groups", "rows"), "vocab"))
    return jax.shard_map(shards, mesh=mesh, in_specs=in_specs, out_specs=out_specs, check_vma=False)
```

profile of v0, /device:TPU:0, one launch (start us, length us, event | category | flops | bytes accessed | tf_op | source)
XLA Modules:
  0.0 124.2 jit_solution(5050734468871903774)
XLA Ops:
  0.7 0.8 compare_select_fusion.8
  1.5 0.8 fusion.43
  2.2 0.8 fusion.44
  3.0 0.8 fusion.45
  3.8 0.1 compare_select_fusion.1
  3.8 0.8 scatter_custom_fusion
  4.6 1.6 %gather_fusion = s32[134]{0:T(256)S(1)} fusion(s32[64]{0:T(128)S(1)} %scatter_custom_fusion, s32[1024]{0:T(1024)S(1)} %pad_clamp_fusion.7), kind=kCustom, calls=%fused_computation | custom fusion | bytes 1608 | tf_op jit(solution)/shard_map/gather | solution.py:77
  6.2 1.0 scatter_custom_fusion.1
  7.2 0.1 reshape.244
  7.3 0.2 reduce_window_sum.11
  7.5 0.1 sub.101
  7.6 1.6 %gather_fusion.1 = s32[134]{0:T(256)S(1)} fusion(s32[64]{0:T(128)S(1)} %sub.101, s32[1024]{0:T(1024)S(1)} %pad_clamp_fusion.6), kind=kCustom, calls=%fused_computation.1 | custom fusion | bytes 1608 | tf_op jit(solution)/shard_map/gather | solution.py:80
  9.2 1.0 scatter_custom_fusion.2
  10.2 0.7 all_to_all.9
  10.9 6.3 %all-to-all-start = ((s32[4,1,4]{2,1,0:T(1,128)}), s32[4,1,4]{2,1,0:T(1,128)S(1)}, u32[]{:S(2)}, u32[]{:S(2)}) async-start(s32[4,1,4]{2,1,0:T(1,128)} %bitcast.5), calls=%async_computation | async-start | bytes 4096 | tf_op jit(solution)/shard_map/all_to_all | solution.py:101
  17.2 0.1 slice.45
  17.3 0.1 slice.42
  17.5 0.3 copy.26
  17.8 0.3 copy.33
  18.1 0.3 copy.28
  18.4 0.3 fusion.10
  18.8 1.6 %copy.30 = bf16[128,4096]{0,1:T(8,128)(2,1)S(1)} copy(bf16[128,4096]{1,0:T(8,128)(2,1)} %param.11) | data formatting | bytes 2097152 | tf_op args[2]
  20.4 0.6 fusion.3
  21.0 0.3 fusion.20
  21.2 12.2 %all-reduce.2 = (f32[128]{0:T(128)S(1)}, f32[128]{0:T(128)S(1)}, f32[128]{0:T(128)S(1)}, f32[128]{0:T(128)S(1)}) all-reduce(f32[128]{0:T(128)S(1)} %get-tuple-element.39, f32[128]{0:T(128)S(1)} %get-tuple-element.40, f32[128]{0:T(128)S(1)} %fusion.10, f32[128]{0:T(128)S(1)} %fusion.3), channel_id=1, replica_groups=mesh['groups'=2,'vocab'=4,'rows'=4] {'vocab'}, use_global_device_ids=true, to_apply=%region_22.23 | all-reduce | flops 512 | bytes 4096 | tf_op jit(solution)/shard_map/pmax | solution.py:71
  33.4 0.3 fusion.23
  33.7 0.3 fusion.11
  34.1 0.6 fusion.4
  34.6 8.5 %all-reduce.1 = (f32[128]{0:T(128)S(1)}, f32[128]{0:T(128)S(1)}, f32[128]{0:T(128)S(1)}) all-reduce(f32[128]{0:T(128)S(1)} %fusion.23, f32[128]{0:T(128)S(1)} %fusion.11, f32[128]{0:T(128)S(1)} %fusion.4), channel_id=1, replica_groups=mesh['groups'=2,'vocab'=4,'rows'=4] {'vocab'}, use_global_device_ids=true, to_apply=%region_7.0 | all-reduce | flops 384 | bytes 3072 | tf_op jit(solution)/shard_map/psum | solution.py:70
  43.2 1.5 %divide_convert_fusion = bf16[128,4096]{0,1:T(8,128)(2,1)} fusion(bf16[128,4096]{0,1:T(8,128)(2,1)S(1)} %copy.30, f32[128]{0:T(128)S(1)} %get-tuple-element.13, f32[128]{0:T(128)S(1)} %get-tuple-element.17), kind=kLoop, calls=%fused_computation.18 | loop fusion | flops 2621440 | bytes 2098176 | tf_op jit(solution)/shard_map/convert_element_type | solution.py:89
  44.7 1.6 %copy.31 = bf16[128,32,128]{2,0,1:T(8,128)(2,1)S(1)} copy(bf16[128,32,128]{0,2,1:T(8,128)(2,1)} %bitcast.75) | data formatting | bytes 2097152 | tf_op jit(solution)/shard_map/reshape | solution.py:91
  46.3 1.0 divide_convert_fusion.2
  47.3 1.1 divide_convert_fusion.1
  48.4 1.4 %copy.29 = bf16[128,19,128]{2,0,1:T(8,128)(2,1)S(1)} copy(bf16[128,19,128]{0,2,1:T(8,128)(2,1)} %bitcast.76) | data formatting | bytes 1245184 | tf_op jit(solution)/shard_map/reshape | solution.py:91
  49.8 1.3 %copy.27 = bf16[128,16,128]{2,0,1:T(8,128)(2,1)S(1)} copy(bf16[128,16,128]{0,2,1:T(8,128)(2,1)} %bitcast.77) | data formatting | bytes 1048576 | tf_op jit(solution)/shard_map/reshape | solution.py:91
  51.2 1.7 %gather_fusion.3 = bf16[32,128,128]{2,1,0:T(8,128)(2,1)} fusion(bf16[16,128,128]{2,1,0:T(8,128)(2,1)S(1)} %copy-done, s32[1024]{0:T(1024)S(1)} %pad_clamp_fusion.4), kind=kCustom, calls=%fused_computation.3 | custom fusion | bytes 2097280 | tf_op jit(solution)/shard_map/jit(_take)/gather | solution.py:93
  52.8 1.8 %gather_fusion.5 = bf16[38,128,128]{2,1,0:T(8,128)(2,1)} fusion(bf16[16,128,128]{2,1,0:T(8,128)(2,1)S(1)} %copy-done, s32[1024]{0:T(1024)S(1)} %pad_clamp_fusion.2), kind=kCustom, calls=%fused_computation.5 | custom fusion | bytes 2490520 | tf_op jit(solution)/shard_map/jit(_take)/gather | solution.py:93
  54.6 2.1 %gather_fusion.7 = bf16[64,128,128]{2,1,0:T(8,128)(2,1)} fusion(bf16[16,128,128]{2,1,0:T(8,128)(2,1)S(1)} %copy-done, s32[1024]{0:T(1024)S(1)} %pad_clamp_fusion), kind=kCustom, calls=%fused_computation.7 | custom fusion | bytes 4194560 | tf_op jit(solution)/shard_map/jit(_take)/gather | solution.py:93
  56.7 1.6 %gather_fusion.2 = bf16[32,128,128]{2,1,0:T(8,128)(2,1)} fusion(bf16[128,16,128]{2,0,1:T(8,128)(2,1)S(1)} %copy.27, s32[1024]{0:T(1024)S(1)} %pad_clamp_fusion.5), kind=kCustom, calls=%fused_computation.2 | custom fusion | bytes 2097280 | tf_op jit(solution)/shard_map/jit(_take)/gather | solution.py:20
  58.4 1.9 %gather_fusion.4 = bf16[38,128,128]{2,1,0:T(8,128)(2,1)} fusion(bf16[128,19,128]{2,0,1:T(8,128)(2,1)S(1)} %copy.29, s32[1024]{0:T(1024)S(1)} %pad_clamp_fusion.3), kind=kCustom, calls=%fused_computation.4 | custom fusion | bytes 2490520 | tf_op jit(solution)/shard_map/jit(_take)/gather | solution.py:20
  60.3 2.2 %gather_fusion.6 = bf16[64,128,128]{2,1,0:T(8,128)(2,1)} fusion(bf16[128,32,128]{2,0,1:T(8,128)(2,1)S(1)} %copy.31, s32[1024]{0:T(1024)S(1)} %pad_clamp_fusion.1), kind=kCustom, calls=%fused_computation.6 | custom fusion | bytes 4194560 | tf_op jit(solution)/shard_map/jit(_take)/gather | solution.py:20
  62.5 3.1 %convolution_multiply_fusion.2 = f32[32,128,128]{2,1,0:T(8,128)} fusion(bf16[32,128,128]{2,1,0:T(8,128)(2,1)} %gather_fusion.2, bf16[32,128,128]{2,1,0:T(8,128)(2,1)S(1)} %copy-done.4, pred[32]{0:T(512)(128)(4,1)S(1)} %get-tuple-element.24, pred[32]{0:T(512)(128)(4,1)S(1)} %get-tuple-element.32), kind=kOutput, calls=%fused_computation.26 | convolution fusion | flops 135790592 | bytes 4194368 | tf_op jit(solution)/shard_map/reb,ebc->erc/dot_general | solution.py:22
  65.6 0.1 broadcast.204.clone
  65.7 4.7 %scatter_fusion = f32[16,128,128]{2,1,0:T(8,128)S(1)} fusion(f32[16,128,128]{2,1,0:T(8,128)S(1)} %broadcast.204.clone, s32[32]{0:T(128)S(1)} %slice.39, f32[32,128,128]{2,1,0:T(8,128)} %convolution_multiply_fusion.2), kind=kCustom, calls=%fused_computation.11 | custom fusion | flops 524288 | bytes 6291584 | tf_op jit(solution)/shard_map/scatter-add | solution.py:25
  70.4 3.7 %convolution_multiply_fusion.1 = f32[38,128,128]{2,1,0:T(8,128)} fusion(bf16[38,128,128]{2,1,0:T(8,128)(2,1)S(1)} %copy-done.3, bf16[38,128,128]{2,1,0:T(8,128)(2,1)} %gather_fusion.5, pred[38]{0:T(512)(128)(4,1)S(1)} %get-tuple-element.22, pred[38]{0:T(512)(128)(4,1)S(1)} %get-tuple-element.29), kind=kOutput, calls=%fused_computation.25 | convolution fusion | flops 161251328 | bytes 4980812 | tf_op jit(solution)/shard_map/reb,ebc->erc/dot_general | solution.py:22
  74.1 0.1 broadcast.204.clone.1
  74.2 6.5 %scatter_fusion.1 = f32[16,128,128]{2,1,0:T(8,128)S(1)} fusion(f32[16,128,128]{2,1,0:T(8,128)S(1)} %broadcast.204.clone.1, s32[38]{0:T(128)S(1)} %slice.42, f32[38,128,128]{2,1,0:T(8,128)} %convolution_multiply_fusion.1), kind=kCustom, calls=%fused_computation.12 | custom fusion | flops 622592 | bytes 7471256 | tf_op jit(solution)/shard_map/scatter-add | solution.py:25
  80.7 1.5 %add.166 = f32[16,128,128]{2,1,0:T(8,128)S(1)} add(f32[16,128,128]{2,1,0:T(8,128)} %copy-done.1, f32[16,128,128]{2,1,0:T(8,128)S(1)} %scatter_fusion.1) | non-fusion elementwise | flops 262144 | bytes 3145728 | tf_op jit(solution)/shard_map/add | solution.py:26
  82.2 0.4 copy-done.2
  82.6 4.4 %convolution_multiply_fusion = f32[64,128,128]{2,1,0:T(8,128)} fusion(bf16[64,128,128]{2,1,0:T(8,128)(2,1)} %gather_fusion.6, bf16[64,128,128]{2,1,0:T(8,128)(2,1)S(1)} %copy-done.2, pred[64]{0:T(512)(128)(4,1)S(1)} %get-tuple-element.20, pred[64]{0:T(512)(128)(4,1)S(1)} %get-tuple-element.26), kind=kOutput, calls=%fused_computation.14 | convolution fusion | flops 271581184 | bytes 8388736 | tf_op jit(solution)/shard_map/reb,ebc->erc/dot_general | solution.py:22
  87.0 8.8 %scatter_fusion.2 = f32[16,128,128]{2,1,0:T(8,128)S(1)} fusion(f32[16,128,128]{2,1,0:T(8,128)S(1)} %add.166, s32[64]{0:T(128)S(1)} %slice.45, f32[64,128,128]{2,1,0:T(8,128)} %convolution_multiply_fusion), kind=kCustom, calls=%fused_computation.13 | custom fusion | flops 1048576 | bytes 12583168 | tf_op jit(solution)/shard_map/scatter-add | solution.py:25
  95.8 0.9 convert_element_type.34
  96.7 3.5 %all-to-all-start.1 = ((bf16[4,4,128,128]{3,2,1,0:T(8,128)(2,1)}), bf16[4,4,128,128]{3,2,1,0:T(8,128)(2,1)S(1)}, u32[]{:S(2)}, u32[]{:S(2)}) async-start(bf16[4,4,128,128]{3,2,1,0:T(8,128)(2,1)} %bitcast.25), calls=%async_computation.1 | async-start | bytes 1048576 | tf_op jit(solution)/shard_map/all_to_all | solution.py:100
  100.2 0.5 broadcast.335
  100.7 0.7 reduce.5
  101.4 0.1 eq.17
  101.5 9.2 %all-to-all-done.1 = bf16[4,4,128,128]{3,2,1,0:T(8,128)(2,1)S(1)} async-done(((bf16[4,4,128,128]{3,2,1,0:T(8,128)(2,1)}), bf16[4,4,128,128]{3,2,1,0:T(8,128)(2,1)S(1)}, u32[]{:S(2)}, u32[]{:S(2)}) %all-to-all-start.1) | async-done | bytes 524320 | tf_op jit(solution)/shard_map/all_to_all | solution.py:100
  110.6 1.2 fusion.46
  111.8 0.4 copy.37
  112.2 0.3 exponential_reduce_fusion
  112.5 9.8 %all-reduce = (f32[128]{0:T(128)S(1)}, f32[128]{0:T(128)S(1)}, f32[128]{0:T(128)S(1)}) all-reduce(f32[128]{0:T(128)S(1)} %get-tuple-element.7, f32[128]{0:T(128)S(1)} %get-tuple-element.37, f32[128]{0:T(128)S(1)} %get-tuple-element.6), channel_id=1, replica_groups=mesh['groups'=2,'vocab'=4,'rows'=4] {'vocab'}, use_global_device_ids=true, to_apply=%region_26.27 | all-reduce | flops 384 | bytes 3072 | tf_op jit(solution)/shard_map/psum | solution.py:107
  122.3 0.5 multiply_subtract_fusion
  122.8 0.3 fusion.16
  123.1 1.0 copy.36
  (40 shorter events, 0.2 us)
Async XLA Ops:
  0.6 50.5 %copy-start = (bf16[16,128,128]{2,1,0:T(8,128)(2,1)S(1)}, bf16[16,128,128]{2,1,0:T(8,128)(2,1)}, u32[]{:S(2)}) copy-start(bf16[16,128,128]{2,1,0:T(8,128)(2,1)} %param.16) | copy-start | bytes 1572868
  0.6 16.7 %copy-start.8 = (s32[32,3]{0,1:T(4,128)S(1)}, s32[32,3]{0,1:T(4,128)}, u32[]{:S(2)}) copy-start(s32[32,3]{0,1:T(4,128)} %param.13) | copy-start | bytes 1156
  0.7 16.7 %copy-start.9 = (s32[38,3]{0,1:T(4,128)S(1)}, s32[38,3]{0,1:T(4,128)}, u32[]{:S(2)}) copy-start(s32[38,3]{0,1:T(4,128)} %param.14) | copy-start | bytes 1372
  0.7 16.7 %copy-start.10 = (s32[64,3]{0,1:T(4,128)S(1)}, s32[64,3]{0,1:T(4,128)}, u32[]{:S(2)}) copy-start(s32[64,3]{0,1:T(4,128)} %param.15) | copy-start | bytes 2308
  0.7 16.8 %copy-start.6 = (bf16[128,2048]{1,0:T(8,128)(2,1)S(1)}, bf16[128,2048]{1,0:T(8,128)(2,1)}, u32[]{:S(2)}) copy-start(bf16[128,2048]{1,0:T(8,128)(2,1)} %param.9) | copy-start | bytes 1572868
  0.7 17.1 %copy-start.7 = (bf16[128,2048]{1,0:T(8,128)(2,1)S(1)}, bf16[128,2048]{1,0:T(8,128)(2,1)}, u32[]{:S(2)}) copy-start(bf16[128,2048]{1,0:T(8,128)(2,1)} %param.12) | copy-start | bytes 1572868
  4.6 13.5 %copy-start.5 = (bf16[128,2432]{1,0:T(8,128)(2,1)S(1)}, bf16[128,2432]{1,0:T(8,128)(2,1)}, u32[]{:S(2)}) copy-start(bf16[128,2432]{1,0:T(8,128)(2,1)} %param.10) | copy-start | bytes 1867780
  10.9 85.8 %all-to-all-start = ((s32[4,1,4]{2,1,0:T(1,128)}), s32[4,1,4]{2,1,0:T(1,128)S(1)}, u32[]{:S(2)}, u32[]{:S(2)}) async-start(s32[4,1,4]{2,1,0:T(1,128)} %bitcast.5), calls=%async_computation | async-start | bytes 4096 | tf_op jit(solution)/shard_map/all_to_all | solution.py:101
  60.3 2.2 %copy-start.4 = (bf16[32,128,128]{2,1,0:T(8,128)(2,1)S(1)}, bf16[32,128,128]{2,1,0:T(8,128)(2,1)}, u32[]{:S(2)}) copy-start(bf16[32,128,128]{2,1,0:T(8,128)(2,1)} %gather_fusion.3) | copy-start | bytes 3145732
  65.7 4.7 %copy-start.3 = (bf16[38,128,128]{2,1,0:T(8,128)(2,1)S(1)}, bf16[38,128,128]{2,1,0:T(8,128)(2,1)}, u32[]{:S(2)}) copy-start(bf16[38,128,128]{2,1,0:T(8,128)(2,1)} %gather_fusion.4) | copy-start | bytes 3735556
  70.4 3.7 %copy-start.1 = (f32[16,128,128]{2,1,0:T(8,128)}, f32[16,128,128]{2,1,0:T(8,128)S(1)}, u32[]{:S(2)}) copy-start(f32[16,128,128]{2,1,0:T(8,128)S(1)} %scatter_fusion) | copy-start | bytes 3145732
  80.7 1.9 %copy-start.2 = (bf16[64,128,128]{2,1,0:T(8,128)(2,1)S(1)}, bf16[64,128,128]{2,1,0:T(8,128)(2,1)}, u32[]{:S(2)}) copy-start(bf16[64,128,128]{2,1,0:T(8,128)(2,1)} %gather_fusion.7) | copy-start | bytes 6291460
  96.7 13.9 %all-to-all-start.1 = ((bf16[4,4,128,128]{3,2,1,0:T(8,128)(2,1)}), bf16[4,4,128,128]{3,2,1,0:T(8,128)(2,1)S(1)}, u32[]{:S(2)}, u32[]{:S(2)}) async-start(bf16[4,4,128,128]{3,2,1,0:T(8,128)(2,1)} %bitcast.25), calls=%async_computation.1 | async-start | bytes 1048576 | tf_op jit(solution)/shard_map/all_to_all | solution.py:100
where the time goes:
time: 125 us; the launch traced here: 124 us
  other arithmetic  33.6 us (27%)
  blocking collectives  30.6 us (24%)
  local copies, waits for them, and re-layouts  27.7 us (22%)
  matrix products  12.4 us (10%)
  starting transfers between devices  9.79 us (8%)
  waiting for transfers between devices  9.15 us (7%)
    scatter-add x3, other arithmetic, slot_sums(): jax.ops.segment_sum(mapped_part, own_slots, num_segments=slots_total)  19.9 us
    pmax x1, blocking collectives, shards(): student_peak = lax.pmax(student_high, 'vocab')  12.2 us
    dot_general x3, matrix products, slot_sums(): jnp.einsum('reb,ebc->erc', picked, tile_rows, preferred_element_type=jnp....  11.2 us
    psum x1, blocking collectives, shards(): lax.psum((total_local, cross_local, student_local), 'vocab')  9.82 us
    all_to_all x1, waiting for transfers between devices, shards(): lax.all_to_all(outgoing, 'vocab', split_axis=0, concat_axis=0, tiled=True)  9.15 us
    psum x1, blocking collectives, shards(): teacher_total = lax.psum((sum_llama, sum_qwen, sum_gemma), 'vocab')  8.54 us
    all_to_all x1, starting transfers between devices, shards(): lax.all_to_all(label_grid, 'vocab', split_axis=0, concat_axis=0, tiled=True)  6.32 us
    gather x3, local copies, waits for them, and re-layouts, slot_sums(): picked = jnp.take(grid, local_block, axis=1)  5.73 us
  transfers between devices with their start and end apart: 2, of which 1 were waited for; matrix products, arithmetic and copies ran while one was open for 48% of the time, Pallas kernels for 0%

commit v1 on v0

v1 whole, which is shorter than its diff:
```python
import functools

import jax
import jax.numpy as jnp
from jax import lax
from jax.experimental import pallas as pl
from jax.experimental.pallas import tpu as pltpu
from jax.sharding import PartitionSpec as P

CAP = 4
TEMP = 2.0
SHARE = 1.0 / 3.0
LANES = 128
MESH = pl.DeviceIdType.MESH


def iota(shape, dim):
    return lax.broadcasted_iota(jnp.int32, shape, dim)


def ones_where(mask):
    return jnp.where(mask, 1, 0)


def peer_of(me, k, n):
    out = 0
    bit = 1
    while bit < n:
        out = out + lax.rem(lax.div(me, bit) + (k // bit) % 2, 2) * bit
        bit *= 2
    return out


def pick_unroll(count):
    return max(u for u in range(1, 21) if count % u == 0)


def to_rows(columns, rows):
    lane = iota((rows, LANES), 1)
    grid = jnp.zeros((rows, LANES), jnp.float32)
    for k, column in enumerate(columns):
        grid = jnp.where(lane == k, column, grid)
    return grid.T[0:8]


def to_columns(row_block):
    return jnp.concatenate([row_block] * (LANES // 8), axis=0).T


def write_tables(n, span, block_counts, me, aligns, order_ref, meta_v, inv_v):
    width = n * span
    order_row = order_ref[...]
    hits = [a[:, 1:2] == order_row for a in aligns]
    present = sum(jnp.sum(ones_where(h), axis=0, keepdims=True) for h in hits)
    present = jnp.minimum(present, 1)
    down, across = iota((width, width), 0), iota((width, width), 1)
    present_col = jnp.sum(jnp.where(down == across, present, 0), axis=1, keepdims=True)
    owner_col = sum((ones_where(iota((width, 1), 0) >= o * span) for o in range(1, n)), jnp.zeros((width, 1), jnp.int32))
    owner_row = sum((ones_where(iota((1, width), 1) >= o * span) for o in range(1, n)), jnp.zeros((1, width), jnp.int32))
    earlier = (down < across) & (owner_col == owner_row)
    rank_row = jnp.sum(jnp.where(earlier, present_col, 0), axis=0, keepdims=True)
    slot_row = owner_row * CAP + rank_row
    inv_v[0] = jnp.zeros(inv_v.shape[1:], jnp.int32)
    meta_v[...] = jnp.zeros(meta_v.shape, jnp.int32)
    inv_v[0, 0:1, 0:width] = jnp.where(present > 0, jnp.minimum(rank_row, CAP), CAP)
    lanes = meta_v.shape[1]
    for t, (a, hit, blocks) in enumerate(zip(aligns, hits, block_counts)):
        count = a.shape[0]
        slot = jnp.sum(jnp.where(hit, slot_row, 0), axis=1, keepdims=True)
        down, across = iota((count, count), 0), iota((count, count), 1)
        slot_lane = jnp.sum(jnp.where(down == across, slot, 0), axis=0, keepdims=True)
        same_before = jnp.sum(
            ones_where((slot_lane == slot) & (across < down)), axis=1, keepdims=True
        )
        rank = same_before + jnp.sum(ones_where(slot_lane < slot), axis=1, keepdims=True)
        lane = iota((count, lanes), 1)
        place = rank == lane

        def by_rank(values):
            return jnp.sum(jnp.where(place, values, 0), axis=0, keepdims=True)

        meta_v[4 * t : 4 * t + 1, :] = by_rank(jnp.clip(a[:, 0:1] - me * blocks, 0, blocks - 1))
        meta_v[4 * t + 1 : 4 * t + 2, :] = by_rank(a[:, 2:3])
        meta_v[4 * t + 2 : 4 * t + 3, :] = by_rank(jnp.minimum(same_before, 1))
        upto = jnp.sum(ones_where(slot <= lane), axis=0, keepdims=True)
        here = jnp.sum(ones_where(slot == lane), axis=0, keepdims=True)
        meta_v[4 * t + 3 : 4 * t + 4, :] = jnp.where(here > 0, upto - 1, count)


def kernel(
    n, llama, qwen, gemma, student, al, aq, ag, tiles_hbm, order_ref,
    loss_ref, grad_ref,
    xl, xq, xg, xs, wl, wq, wg, pl_, pq, pg, tiles, meta_v, meta_s, inv_v, inv_s,
    stat, tot, crs, send, recv, in_sem, smem_sem, snd, rcv,
):
    me = lax.axis_index("vocab")
    rows = xs.shape[0]
    span = xs.shape[1] // LANES
    peers = [peer_of(me, k, n) for k in range(n)]
    order = [k for k in range(n - 1, 0, -1)]
    order.sort(key=lambda k: (k < n // 2, k))
    factor = n * span * LANES / TEMP

    raw = [xl, xq, xg]
    weights = [wl, wq, wg]
    prefix = [pl_, pq, pg]
    loads = [
        pltpu.make_async_copy(src, dst, in_sem.at[i])
        for i, (src, dst) in enumerate(
            [(llama, xl), (qwen, xq), (gemma, xg), (student, xs), (tiles_hbm, tiles)]
        )
    ]
    for load in loads:
        load.start()
    barrier = pltpu.get_barrier_semaphore()
    for k in range(1, n):
        pl.semaphore_signal(barrier, inc=1, device_id={"vocab": peers[k]}, device_id_type=MESH)

    aligns = [al[...], aq[...], ag[...]]
    block_counts = [x.shape[1] // LANES for x in raw]
    write_tables(n, span, block_counts, me, aligns, order_ref, meta_v, inv_v)
    meta_copy = pltpu.make_async_copy(meta_v, meta_s, smem_sem.at[0])
    meta_copy.start()
    for t in range(3):
        prefix[t][aligns[t].shape[0]] = jnp.zeros((rows, LANES), jnp.float32)
    for k in range(n):
        recv[k, CAP] = jnp.zeros((rows, LANES), jnp.bfloat16)

    def local_stats(x, w):
        blocks = x.shape[1] // LANES
        top = x[:, 0:LANES]
        for b in range(1, blocks):
            top = jnp.maximum(top, x[:, b * LANES : (b + 1) * LANES])
        top = jnp.max(top.astype(jnp.float32), axis=1, keepdims=True) / TEMP
        total = jnp.zeros((rows, LANES), jnp.float32)
        for b in range(blocks):
            e = jnp.exp(x[:, b * LANES : (b + 1) * LANES].astype(jnp.float32) / TEMP - top)
            total = total + e
            if w is not None:
                w[b] = e.astype(jnp.bfloat16)
        return top, jnp.sum(total, axis=1, keepdims=True)

    stats = []
    for t in range(3):
        loads[t].wait()
        stats.extend(local_stats(raw[t], weights[t]))
    loads[3].wait()
    stats.extend(local_stats(xs, None))
    stat[0] = to_rows(stats, rows)

    pl.semaphore_wait(barrier, n - 1)

    def remote(src, dst, kind, k):
        return pltpu.make_async_remote_copy(
            src_ref=src, dst_ref=dst, send_sem=snd.at[kind, k], recv_sem=rcv.at[kind, k],
            device_id={"vocab": peers[k]}, device_id_type=MESH,
        )

    stat_copies = [remote(stat.at[0], stat.at[k], 0, k) for k in order]
    inv_copies = [remote(inv_v.at[0], inv_v.at[k], 1, k) for k in order]
    for c in stat_copies + inv_copies:
        c.start()

    meta_copy.wait()
    loads[4].wait()
    for t in range(3):
        count = aligns[t].shape[0]
        unroll = pick_unroll(count)

        def step(i, acc, t=t, unroll=unroll):
            for u in range(unroll):
                p = i * unroll + u
                product = jnp.dot(
                    weights[t][meta_s[4 * t, p]],
                    tiles[meta_s[4 * t + 1, p]],
                    preferred_element_type=jnp.float32,
                )
                acc = jnp.where(meta_s[4 * t + 2, p] > 0, acc, 0.0) + product
                prefix[t][p] = acc
            return acc

        lax.fori_loop(0, count // unroll, step, jnp.zeros((rows, LANES), jnp.float32))

    for c in stat_copies:
        c.wait()
    mine = stat[0]
    scale_rows = []
    lse_row = None
    for t in range(4):
        peak = mine[2 * t : 2 * t + 1]
        for k in range(1, n):
            peak = jnp.maximum(peak, stat[k, 2 * t : 2 * t + 1])
        whole = jnp.zeros((1, rows), jnp.float32)
        for k in range(n):
            whole = whole + stat[k, 2 * t + 1 : 2 * t + 2] * jnp.exp(stat[k, 2 * t : 2 * t + 1] - peak)
        if t < 3:
            scale_rows.append(jnp.exp(mine[2 * t : 2 * t + 1] - peak) / whole * SHARE)
        else:
            lse_row = peak + jnp.log(whole)
    packed = to_columns(jnp.concatenate(scale_rows + [lse_row] + [jnp.zeros((4, rows), jnp.float32)], axis=0))
    scales = [packed[:, t : t + 1] for t in range(3)]
    lse = packed[:, 3:4]

    row_sum = jnp.zeros((rows, LANES), jnp.float32)
    data_copies = []
    for k in order + [0]:
        for j in range(CAP):
            s = peers[k] * CAP + j
            part = scales[0] * prefix[0][meta_s[3, s]]
            part = part + scales[1] * prefix[1][meta_s[7, s]]
            part = part + scales[2] * prefix[2][meta_s[11, s]]
            part = part.astype(jnp.bfloat16)
            row_sum = row_sum + part.astype(jnp.float32)
            if k == 0:
                recv[0, j] = part
            else:
                send[k, j] = part
        if k != 0:
            c = remote(send.at[k], recv.at[k, pl.ds(0, CAP)], 2, k)
            c.start()
            data_copies.append(c)
    tot[0] = to_rows([jnp.sum(row_sum, axis=1, keepdims=True)], rows)
    tot_copies = [remote(tot.at[0], tot.at[k], 3, k) for k in order]
    for c in tot_copies:
        c.start()
    for c in inv_copies:
        c.wait()
    inv_copy = pltpu.make_async_copy(inv_v, inv_s, smem_sem.at[1])
    inv_copy.start()
    inv_copy.wait()
    for c in tot_copies:
        c.wait()
    total_rows = sum(tot[k] for k in range(n))
    total = to_columns(total_rows)[:, 0:1]
    for c in data_copies:
        c.wait()

    cross = jnp.zeros((rows, LANES), jnp.float32)
    for b in range(span):
        target = jnp.zeros((rows, LANES), jnp.float32)
        for k in range(n):
            target = target + recv[k, inv_s[k, 0, me * span + b]].astype(jnp.float32)
        cols = slice(b * LANES, (b + 1) * LANES)
        scaled = xs[:, cols].astype(jnp.float32) / TEMP
        cross = cross + target * scaled
        grad_ref[:, cols] = (factor * (total * jnp.exp(scaled - lse) - target)).astype(jnp.bfloat16)
    crs[0] = to_rows([jnp.sum(cross, axis=1, keepdims=True)], rows)
    cross_copies = [remote(crs.at[0], crs.at[k], 4, k) for k in order]
    for c in cross_copies:
        c.start()
    for c in cross_copies:
        c.wait()
    cross_rows = sum(crs[k] for k in range(n))
    loss_ref[...] = total_rows[0:1] * lse_row - cross_rows[0:1]


def shards(llama, qwen, gemma, student, al, aq, ag, tiles, student_order):
    n = lax.axis_size("vocab")
    rows = student.shape[0]
    width = student_order.shape[0]
    aligns = (al, aq, ag)
    most = max([a.shape[0] for a in aligns] + [n * CAP])
    lanes = -(-most // LANES) * LANES
    inv_lanes = -(-width // LANES) * LANES
    logits = (llama, qwen, gemma, student)
    bf16, f32, i32 = jnp.bfloat16, jnp.float32, jnp.int32
    scratch = [pltpu.VMEM(x.shape, bf16) for x in logits]
    scratch += [pltpu.VMEM((x.shape[1] // LANES, rows, LANES), bf16) for x in logits[:3]]
    scratch += [pltpu.VMEM((a.shape[0] + 1, rows, LANES), f32) for a in aligns]
    scratch += [
        pltpu.VMEM(tiles.shape, bf16),
        pltpu.VMEM((16, lanes), i32),
        pltpu.SMEM((16, lanes), i32),
        pltpu.VMEM((n, 8, inv_lanes), i32),
        pltpu.SMEM((n, 8, inv_lanes), i32),
        pltpu.VMEM((n, 8, rows), f32),
        pltpu.VMEM((n, 8, rows), f32),
        pltpu.VMEM((n, 8, rows), f32),
        pltpu.VMEM((n, CAP, rows, LANES), bf16),
        pltpu.VMEM((n, CAP + 1, rows, LANES), bf16),
        pltpu.SemaphoreType.DMA((5,)),
        pltpu.SemaphoreType.DMA((2,)),
        pltpu.SemaphoreType.DMA((5, n)),
        pltpu.SemaphoreType.DMA((5, n)),
    ]
    hbm = pl.BlockSpec(memory_space=pl.ANY)
    vmem = pl.BlockSpec(memory_space=pltpu.VMEM)
    loss, grad = pl.pallas_call(
        functools.partial(kernel, n),
        out_shape=(
            jax.ShapeDtypeStruct((1, rows), f32),
            jax.ShapeDtypeStruct(student.shape, bf16),
        ),
        in_specs=[hbm] * 4 + [vmem] * 3 + [hbm, vmem],
        out_specs=(vmem, vmem),
        scratch_shapes=scratch,
        compiler_params=pltpu.CompilerParams(
            collective_id=0, has_side_effects=True, vmem_limit_bytes=52 * 2**20
        ),
    )(llama, qwen, gemma, student, al, aq, ag, tiles, student_order.reshape(1, width))
    return loss.reshape(rows), grad


def solution(mesh):
    wide = P(("groups", "rows"), "vocab")
    in_specs = (wide, wide, wide, wide, P("vocab", None), P("vocab", None), P("vocab", None), P(), P())
    out_specs = (P(("groups", "rows")), wide)
    return jax.shard_map(shards, mesh=mesh, in_specs=in_specs, out_specs=out_specs, check_vma=False)
```

time: 125 us -> 33.3 us (0.27)
  other arithmetic: 33.6 us -> 0 us
  blocking collectives: 30.6 us -> 0 us
  Pallas kernels: 0 us -> 26.9 us
  local copies, waits for them, and re-layouts: 27.7 us -> 5.5 us
  matrix products: 12.4 us -> 0 us
  starting transfers between devices: 9.79 us -> 0 us
  waiting for transfers between devices: 9.15 us -> 0 us
    pallas_call x0 -> x1, Pallas kernels: none -> 26.9 us  [shards(): pl.pallas_call(functools.partial(kernel, n), out_shape=(jax.ShapeDtypeStr...]
    scatter-add x3 -> x0, other arithmetic: 19.9 us -> none  [slot_sums(): jax.ops.segment_sum(mapped_part, own_slots, num_segments=slots_total)]
    psum x2 -> x0, blocking collectives: 18.4 us -> none  [the longest x1 9.82 us: shards(): lax.psum((total_local, cross_local, student_local), 'vocab')]
    gather x8 -> x0, local copies, waits for them, and re-layouts: 14.4 us -> none  [the longest x3 5.73 us: slot_sums(): picked = jnp.take(grid, local_block, axis=1)]
    dot_general x4 -> x0, matrix products: 12.4 us -> none  [the longest x3 11.2 us: slot_sums(): jnp.einsum('reb,ebc->erc', picked, tile_rows, preferred_element_type=jnp....]
    pmax x1 -> x0, blocking collectives: 12.2 us -> none  [shards(): student_peak = lax.pmax(student_high, 'vocab')]
    all_to_all x2 -> x0, starting transfers between devices: 9.79 us -> none  [the longest x1 6.32 us: shards(): lax.all_to_all(label_grid, 'vocab', split_axis=0, concat_axis=0, tiled=True)]
    all_to_all x2 -> x0, waiting for transfers between devices: 9.15 us -> none  [the longest x1 9.15 us: shards(): lax.all_to_all(outgoing, 'vocab', split_axis=0, concat_axis=0, tiled=True)]
  transfers between devices with their start and end apart: 2 -> 0, of which waited for: 1 -> 0; matrix products, arithmetic and copies ran while one was open for 48% -> 0% of each run, Pallas kernels for 0% -> 0%
where the time goes in v1:
time: 33.3 us; the launch traced here: 33 us
  Pallas kernels  26.9 us (81%)
  local copies, waits for them, and re-layouts  5.5 us (17%)
  between operations  0.65 us (2%)
    pallas_call x1, Pallas kernels, shards(): pl.pallas_call(functools.partial(kernel, n), out_shape=(jax.ShapeDtypeStr...  26.9 us
    unnamed x15, local copies, waits for them, and re-layouts  5.5 us

profile of v1, /device:TPU:0, one launch (start us, length us, event | category | flops | bytes accessed | tf_op | source)
XLA Modules:
  0.0 33.0 jit_solution(8627784883393309670)
XLA Ops:
  0.6 0.0 copy-start.4
  0.6 0.8 %copy.11.al = s32[32,3]{1,0:T(8,128)S(1)} copy(s32[32,3]{0,1:T(4,128)} %param.13) | data formatting | bytes 768 | tf_op args[4]
  1.4 0.0 copy-done.4
  1.4 0.0 copy-start.3
  1.4 0.1 copy.12.aq
  1.5 0.6 %copy-done.3 = s32[64,3]{0,1:T(4,128)S(1)} copy-done((s32[64,3]{0,1:T(4,128)S(1)}, s32[64,3]{0,1:T(4,128)}, u32[]{:S(2)}) %copy-start.3) | copy-done | bytes 792
  2.1 0.0 copy-start.2
  2.1 0.1 copy.13.ag
  2.2 0.6 %copy-done.2 = s32[64]{0:T(128)S(1)} copy-done((s32[64]{0:T(128)S(1)}, s32[64]{0:T(128)}, u32[]{:S(2)}) %copy-start.2) | copy-done | bytes 280
  2.7 0.0 copy-start
  2.8 1.0 %copy-done = bf16[128,2048]{1,0:T(8,128)(2,1)S(1)} copy-done((bf16[128,2048]{1,0:T(8,128)(2,1)S(1)}, bf16[128,2048]{1,0:T(8,128)(2,1)}, u32[]{:S(2)}) %copy-start) | copy-done | bytes 524312
  3.8 0.0 copy-start.1
  3.8 1.0 %copy-done.1 = bf16[128,2048]{1,0:T(8,128)(2,1)S(1)} copy-done((bf16[128,2048]{1,0:T(8,128)(2,1)S(1)}, bf16[128,2048]{1,0:T(8,128)(2,1)}, u32[]{:S(2)}) %copy-start.1) | copy-done | bytes 524312
  4.8 26.9 %shard_map.104 = (f32[1,128]{1,0:T(1,128)S(1)}, bf16[128,2048]{1,0:T(8,128)(2,1)S(1)}) custom-call(bf16[128,2048]{1,0:T(8,128)(2,1)S(1)} %copy-done, bf16[128,2432]{1,0:T(8,128)(2,1)} %qwen.1, bf16[128,4096]{1,0:T(8,128)(2,1)} %gemma.1, bf16[128,2048]{1,0:T(8,128)(2,1)S(1)} %copy-done.1, s32[32,3]{1,0:T(8,128)S(1)} %copy.11.al, s32[38,3]{1,0:T(8,128)S(1)} %copy.12.aq, ...), custom_call_target="tpu_custom_call" | custom-call | tf_op jit(solution)/shard_map/pallas_call | solution.py:288
  31.7 0.5 %copy.16 = f32[128]{0:T(128)} copy(f32[128]{0:T(128)S(1)} %bitcast.3) | data formatting | bytes 1024
  32.2 0.8 %copy.17 = bf16[128,2048]{1,0:T(8,128)(2,1)} copy(bf16[128,2048]{1,0:T(8,128)(2,1)S(1)} %get-tuple-element.9) | data formatting | bytes 1048576
Async XLA Ops:
  0.6 0.8 %copy-start.4 = (s32[38,3]{0,1:T(4,128)S(1)}, s32[38,3]{0,1:T(4,128)}, u32[]{:S(2)}) copy-start(s32[38,3]{0,1:T(4,128)} %param.14) | copy-start | bytes 1372
  1.4 0.7 %copy-start.3 = (s32[64,3]{0,1:T(4,128)S(1)}, s32[64,3]{0,1:T(4,128)}, u32[]{:S(2)}) copy-start(s32[64,3]{0,1:T(4,128)} %param.15) | copy-start | bytes 2308
  2.1 0.7 %copy-start.2 = (s32[64]{0:T(128)S(1)}, s32[64]{0:T(128)}, u32[]{:S(2)}) copy-start(s32[64]{0:T(128)} %param.17) | copy-start | bytes 772
  2.7 1.0 %copy-start = (bf16[128,2048]{1,0:T(8,128)(2,1)S(1)}, bf16[128,2048]{1,0:T(8,128)(2,1)}, u32[]{:S(2)}) copy-start(bf16[128,2048]{1,0:T(8,128)(2,1)} %llama.1) | copy-start | bytes 1572868
  3.8 1.0 %copy-start.1 = (bf16[128,2048]{1,0:T(8,128)(2,1)S(1)}, bf16[128,2048]{1,0:T(8,128)(2,1)}, u32[]{:S(2)}) copy-start(bf16[128,2048]{1,0:T(8,128)(2,1)} %student.1) | copy-start | bytes 1572868

commit v2 on v1

--- a/solution.py
+++ b/solution.py
@@ -47,10 +47,17 @@
     return jnp.concatenate([row_block] * (LANES // 8), axis=0).T
 
 
+def column_of(row):
+    count = row.shape[1]
+    square = (count, count)
+    return jnp.sum(jnp.where(iota(square, 0) == iota(square, 1), row, 0), axis=1, keepdims=True)
+
+
 def write_tables(n, span, block_counts, me, aligns, order_ref, meta_v, inv_v):
     width = n * span
     order_row = order_ref[...]
-    hits = [a[:, 1:2] == order_row for a in aligns]
+    entries = [[column_of(a[f : f + 1, :]) for f in range(3)] for a in aligns]
+    hits = [e[1] == order_row for e in entries]
     present = sum(jnp.sum(ones_where(h), axis=0, keepdims=True) for h in hits)
     present = jnp.minimum(present, 1)
     down, across = iota((width, width), 0), iota((width, width), 1)
@@ -64,8 +71,8 @@
     meta_v[...] = jnp.zeros(meta_v.shape, jnp.int32)
     inv_v[0, 0:1, 0:width] = jnp.where(present > 0, jnp.minimum(rank_row, CAP), CAP)
     lanes = meta_v.shape[1]
-    for t, (a, hit, blocks) in enumerate(zip(aligns, hits, block_counts)):
-        count = a.shape[0]
+    for t, (entry, hit, blocks) in enumerate(zip(entries, hits, block_counts)):
+        count = hit.shape[0]
         slot = jnp.sum(jnp.where(hit, slot_row, 0), axis=1, keepdims=True)
         down, across = iota((count, count), 0), iota((count, count), 1)
         slot_lane = jnp.sum(jnp.where(down == across, slot, 0), axis=0, keepdims=True)
@@ -79,8 +86,8 @@
         def by_rank(values):
             return jnp.sum(jnp.where(place, values, 0), axis=0, keepdims=True)
 
-        meta_v[4 * t : 4 * t + 1, :] = by_rank(jnp.clip(a[:, 0:1] - me * blocks, 0, blocks - 1))
-        meta_v[4 * t + 1 : 4 * t + 2, :] = by_rank(a[:, 2:3])
+        meta_v[4 * t : 4 * t + 1, :] = by_rank(jnp.clip(entry[0] - me * blocks, 0, blocks - 1))
+        meta_v[4 * t + 1 : 4 * t + 2, :] = by_rank(entry[2])
         meta_v[4 * t + 2 : 4 * t + 3, :] = by_rank(jnp.minimum(same_before, 1))
         upto = jnp.sum(ones_where(slot <= lane), axis=0, keepdims=True)
         here = jnp.sum(ones_where(slot == lane), axis=0, keepdims=True)
@@ -88,11 +95,13 @@
 
 
 def kernel(
-    n, llama, qwen, gemma, student, al, aq, ag, tiles_hbm, order_ref,
+    n, llama, qwen, gemma, student, al_hbm, aq_hbm, ag_hbm, tiles_hbm, order_hbm,
     loss_ref, grad_ref,
-    xl, xq, xg, xs, wl, wq, wg, pl_, pq, pg, tiles, meta_v, meta_s, inv_v, inv_s,
-    stat, tot, crs, send, recv, in_sem, smem_sem, snd, rcv,
+    al, aq, ag, order_ref, xl, xq, xg, xs, wl, wq, wg, pl_, pq, pg, tiles, meta_v, meta_s, inv_v, inv_s,
+    stat, tot, crs, target, soft, send, *more,
 ):
+    recv = more[:n]
+    in_sem, smem_sem, snd, rcv = more[n:]
     me = lax.axis_index("vocab")
     rows = xs.shape[0]
     span = xs.shape[1] // LANES
@@ -107,14 +116,20 @@
     loads = [
         pltpu.make_async_copy(src, dst, in_sem.at[i])
         for i, (src, dst) in enumerate(
-            [(llama, xl), (qwen, xq), (gemma, xg), (student, xs), (tiles_hbm, tiles)]
+            [
+                (al_hbm, al), (aq_hbm, aq), (ag_hbm, ag), (order_hbm, order_ref),
+                (llama, xl), (qwen, xq), (gemma, xg), (student, xs), (tiles_hbm, tiles),
+            ]
         )
     ]
-    for load in loads:
-        load.start()
     barrier = pltpu.get_barrier_semaphore()
     for k in range(1, n):
         pl.semaphore_signal(barrier, inc=1, device_id={"vocab": peers[k]}, device_id_type=MESH)
+    for load in loads:
+        load.start()
+    for load in loads[:4]:
+        load.wait()
+    loads = loads[4:]
 
     aligns = [al[...], aq[...], ag[...]]
     block_counts = [x.shape[1] // LANES for x in raw]
@@ -122,9 +137,9 @@
     meta_copy = pltpu.make_async_copy(meta_v, meta_s, smem_sem.at[0])
     meta_copy.start()
     for t in range(3):
-        prefix[t][aligns[t].shape[0]] = jnp.zeros((rows, LANES), jnp.float32)
+        prefix[t][aligns[t].shape[1]] = jnp.zeros((rows, LANES), jnp.float32)
     for k in range(n):
-        recv[k, CAP] = jnp.zeros((rows, LANES), jnp.bfloat16)
+        recv[k][CAP] = jnp.zeros((rows, LANES), jnp.bfloat16)
 
     def local_stats(x, w):
         blocks = x.shape[1] // LANES
@@ -144,8 +159,6 @@
     for t in range(3):
         loads[t].wait()
         stats.extend(local_stats(raw[t], weights[t]))
-    loads[3].wait()
-    stats.extend(local_stats(xs, None))
     stat[0] = to_rows(stats, rows)
 
     pl.semaphore_wait(barrier, n - 1)
@@ -161,10 +174,12 @@
     for c in stat_copies + inv_copies:
         c.start()
 
+    loads[3].wait()
+    student_stats = local_stats(xs, None)
     meta_copy.wait()
     loads[4].wait()
     for t in range(3):
-        count = aligns[t].shape[0]
+        count = aligns[t].shape[1]
         unroll = pick_unroll(count)
 
         def step(i, acc, t=t, unroll=unroll):
@@ -183,23 +198,22 @@
 
     for c in stat_copies:
         c.wait()
-    mine = stat[0]
-    scale_rows = []
-    lse_row = None
-    for t in range(4):
-        peak = mine[2 * t : 2 * t + 1]
+
+    def combine(ref, at):
+        peak = ref[0, at : at + 1]
         for k in range(1, n):
-            peak = jnp.maximum(peak, stat[k, 2 * t : 2 * t + 1])
+            peak = jnp.maximum(peak, ref[k, at : at + 1])
         whole = jnp.zeros((1, rows), jnp.float32)
         for k in range(n):
-            whole = whole + stat[k, 2 * t + 1 : 2 * t + 2] * jnp.exp(stat[k, 2 * t : 2 * t + 1] - peak)
-        if t < 3:
-            scale_rows.append(jnp.exp(mine[2 * t : 2 * t + 1] - peak) / whole * SHARE)
-        else:
-            lse_row = peak + jnp.log(whole)
-    packed = to_columns(jnp.concatenate(scale_rows + [lse_row] + [jnp.zeros((4, rows), jnp.float32)], axis=0))
+            whole = whole + ref[k, at + 1 : at + 2] * jnp.exp(ref[k, at : at + 1] - peak)
+        return peak, whole
+
+    scale_rows = []
+    for t in range(3):
+        peak, whole = combine(stat, 2 * t)
+        scale_rows.append(jnp.exp(stat[0, 2 * t : 2 * t + 1] - peak) / whole * SHARE)
+    packed = to_columns(jnp.concatenate(scale_rows + [jnp.zeros((5, rows), jnp.float32)], axis=0))
     scales = [packed[:, t : t + 1] for t in range(3)]
-    lse = packed[:, 3:4]
 
     row_sum = jnp.zeros((rows, LANES), jnp.float32)
     data_copies = []
@@ -212,14 +226,14 @@
             part = part.astype(jnp.bfloat16)
             row_sum = row_sum + part.astype(jnp.float32)
             if k == 0:
-                recv[0, j] = part
+                recv[0][j] = part
             else:
                 send[k, j] = part
         if k != 0:
-            c = remote(send.at[k], recv.at[k, pl.ds(0, CAP)], 2, k)
+            c = remote(send.at[k], recv[k].at[pl.ds(0, CAP)], 2, k)
             c.start()
             data_copies.append(c)
-    tot[0] = to_rows([jnp.sum(row_sum, axis=1, keepdims=True)], rows)
+    tot[0] = to_rows([*student_stats, jnp.sum(row_sum, axis=1, keepdims=True)], rows)
     tot_copies = [remote(tot.at[0], tot.at[k], 3, k) for k in order]
     for c in tot_copies:
         c.start()
@@ -228,30 +242,39 @@
     inv_copy = pltpu.make_async_copy(inv_v, inv_s, smem_sem.at[1])
     inv_copy.start()
     inv_copy.wait()
+
+    def columns(b):
+        return slice(b * LANES, (b + 1) * LANES)
+
+    def land(k, cross):
+        for b in range(span):
+            block = recv[k][inv_s[k, 0, me * span + b]].astype(jnp.float32)
+            cross = cross + block * (xs[:, columns(b)].astype(jnp.float32) / TEMP)
+            target[b] = block if k == 0 else target[b] + block
+        return cross
+
+    cross = land(0, jnp.zeros((rows, LANES), jnp.float32))
     for c in tot_copies:
         c.wait()
-    total_rows = sum(tot[k] for k in range(n))
-    total = to_columns(total_rows)[:, 0:1]
-    for c in data_copies:
-        c.wait()
-
-    cross = jnp.zeros((rows, LANES), jnp.float32)
+    student_peak, student_total = combine(tot, 0)
+    lse_row = student_peak + jnp.log(student_total)
+    total_row = sum(tot[k, 2:3] for k in range(n))
+    packed = to_columns(jnp.concatenate([lse_row, total_row, jnp.zeros((6, rows), jnp.float32)], axis=0))
+    lse, total = packed[:, 0:1], packed[:, 1:2]
     for b in range(span):
-        target = jnp.zeros((rows, LANES), jnp.float32)
-        for k in range(n):
-            target = target + recv[k, inv_s[k, 0, me * span + b]].astype(jnp.float32)
-        cols = slice(b * LANES, (b + 1) * LANES)
-        scaled = xs[:, cols].astype(jnp.float32) / TEMP
-        cross = cross + target * scaled
-        grad_ref[:, cols] = (factor * (total * jnp.exp(scaled - lse) - target)).astype(jnp.bfloat16)
+        soft[b] = total * jnp.exp(xs[:, columns(b)].astype(jnp.float32) / TEMP - lse)
+    for k, c in zip(order, data_copies):
+        c.wait()
+        cross = land(k, cross)
     crs[0] = to_rows([jnp.sum(cross, axis=1, keepdims=True)], rows)
     cross_copies = [remote(crs.at[0], crs.at[k], 4, k) for k in order]
     for c in cross_copies:
         c.start()
+    for b in range(span):
+        grad_ref[:, columns(b)] = (factor * (soft[b] - target[b])).astype(jnp.bfloat16)
     for c in cross_copies:
         c.wait()
-    cross_rows = sum(crs[k] for k in range(n))
-    loss_ref[...] = total_rows[0:1] * lse_row - cross_rows[0:1]
+    loss_ref[...] = total_row * lse_row - sum(crs[k, 0:1] for k in range(n))
 
 
 def shards(llama, qwen, gemma, student, al, aq, ag, tiles, student_order):
@@ -264,7 +287,8 @@
     inv_lanes = -(-width // LANES) * LANES
     logits = (llama, qwen, gemma, student)
     bf16, f32, i32 = jnp.bfloat16, jnp.float32, jnp.int32
-    scratch = [pltpu.VMEM(x.shape, bf16) for x in logits]
+    scratch = [pltpu.VMEM(a.shape[::-1], i32) for a in aligns] + [pltpu.VMEM((1, width), i32)]
+    scratch += [pltpu.VMEM(x.shape, bf16) for x in logits]
     scratch += [pltpu.VMEM((x.shape[1] // LANES, rows, LANES), bf16) for x in logits[:3]]
     scratch += [pltpu.VMEM((a.shape[0] + 1, rows, LANES), f32) for a in aligns]
     scratch += [
@@ -276,14 +300,18 @@
         pltpu.VMEM((n, 8, rows), f32),
         pltpu.VMEM((n, 8, rows), f32),
         pltpu.VMEM((n, 8, rows), f32),
+        pltpu.VMEM((student.shape[1] // LANES, rows, LANES), f32),
+        pltpu.VMEM((student.shape[1] // LANES, rows, LANES), f32),
         pltpu.VMEM((n, CAP, rows, LANES), bf16),
-        pltpu.VMEM((n, CAP + 1, rows, LANES), bf16),
-        pltpu.SemaphoreType.DMA((5,)),
+    ]
+    scratch += [pltpu.VMEM((CAP + 1, rows, LANES), bf16) for _ in range(n)]
+    scratch += [
+        pltpu.SemaphoreType.DMA((9,)),
         pltpu.SemaphoreType.DMA((2,)),
         pltpu.SemaphoreType.DMA((5, n)),
         pltpu.SemaphoreType.DMA((5, n)),
     ]
-    hbm = pl.BlockSpec(memory_space=pl.ANY)
+    hbm = pl.BlockSpec(memory_space=pltpu.HBM)
     vmem = pl.BlockSpec(memory_space=pltpu.VMEM)
     loss, grad = pl.pallas_call(
         functools.partial(kernel, n),
@@ -291,13 +319,13 @@
             jax.ShapeDtypeStruct((1, rows), f32),
             jax.ShapeDtypeStruct(student.shape, bf16),
         ),
-        in_specs=[hbm] * 4 + [vmem] * 3 + [hbm, vmem],
+        in_specs=[hbm] * 9,
         out_specs=(vmem, vmem),
         scratch_shapes=scratch,
         compiler_params=pltpu.CompilerParams(
-            collective_id=0, has_side_effects=True, vmem_limit_bytes=52 * 2**20
+            collective_id=0, has_side_effects=True, vmem_limit_bytes=60 * 2**20
         ),
-    )(llama, qwen, gemma, student, al, aq, ag, tiles, student_order.reshape(1, width))
+    )(llama, qwen, gemma, student, al.T, aq.T, ag.T, tiles, student_order.reshape(1, width))
     return loss.reshape(rows), grad
 
 

time: 33.3 us -> 32.1 us (0.964)
  local copies, waits for them, and re-layouts: 5.5 us -> 3.05 us
  Pallas kernels: 26.9 us -> 28.2 us
    unnamed x15 -> x4, local copies, waits for them, and re-layouts: 5.5 us -> 3.05 us
    pallas_call x1, Pallas kernels: 26.9 us -> 28.2 us  [shards(): pl.pallas_call(functools.partial(kernel, n), out_shape=(jax.ShapeDtypeStr...]
where the time goes in v2:
time: 32.1 us; the launch traced here: 31.9 us
  Pallas kernels  28.2 us (88%)
  local copies, waits for them, and re-layouts  3.05 us (10%)
  between operations  0.65 us (2%)
    pallas_call x1, Pallas kernels, shards(): pl.pallas_call(functools.partial(kernel, n), out_shape=(jax.ShapeDtypeStr...  28.2 us
    unnamed x4, local copies, waits for them, and re-layouts  3.05 us

profile of v2, /device:TPU:0, one launch (start us, length us, event | category | flops | bytes accessed | tf_op | source)
XLA Modules:
  0.0 31.9 jit_solution(9924472459820926754)
XLA Ops:
  0.6 28.2 %shard_map.104 = (f32[1,128]{1,0:T(1,128)}, bf16[128,2048]{1,0:T(8,128)(2,1)}) custom-call(bf16[128,2048]{1,0:T(8,128)(2,1)} %llama.1, bf16[128,2432]{1,0:T(8,128)(2,1)} %qwen.1, bf16[128,4096]{1,0:T(8,128)(2,1)} %gemma.1, bf16[128,2048]{1,0:T(8,128)(2,1)} %student.1, s32[3,32]{1,0:T(4,128)} %bitcast.5, s32[3,38]{1,0:T(4,128)} %bitcast.6, s32[3,64]{1,0:T(4,128)} %bitcast.7, ...), custom_call_target="tpu_custom_call" | custom-call | tf_op jit(solution)/shard_map/pallas_call | solution.py:316
  28.9 0.0 copy-start
  28.9 0.7 %copy-done = f32[1,128]{1,0:T(1,128)S(1)} copy-done((f32[1,128]{1,0:T(1,128)S(1)}, f32[1,128]{1,0:T(1,128)}, u32[]{:S(2)}) %copy-start) | copy-done | bytes 536
  29.5 0.5 %copy.13 = f32[128]{0:T(128)} copy(f32[128]{0:T(128)S(1)} %bitcast.9) | data formatting | bytes 1024
  30.1 1.9 %copy.14 = bf16[128,2048]{1,0:T(8,128)(2,1)} copy(bf16[128,2048]{1,0:T(8,128)(2,1)} %get-tuple-element.9) | data formatting | bytes 1048576
Async XLA Ops:
  28.9 0.7 %copy-start = (f32[1,128]{1,0:T(1,128)S(1)}, f32[1,128]{1,0:T(1,128)}, u32[]{:S(2)}) copy-start(f32[1,128]{1,0:T(1,128)} %get-tuple-element.4) | copy-start | bytes 1540

commit v3 on v2

--- a/solution.py
+++ b/solution.py
@@ -316,8 +316,8 @@
     loss, grad = pl.pallas_call(
         functools.partial(kernel, n),
         out_shape=(
-            jax.ShapeDtypeStruct((1, rows), f32),
-            jax.ShapeDtypeStruct(student.shape, bf16),
+            pltpu.VMEM((1, rows), f32),
+            pltpu.VMEM(student.shape, bf16),
         ),
         in_specs=[hbm] * 9,
         out_specs=(vmem, vmem),

time: 32.1 us -> 29.5 us (0.919)
  local copies, waits for them, and re-layouts: 3.05 us -> 1.31 us
  Pallas kernels: 28.2 us -> 27.4 us
    unnamed x4 -> x2, local copies, waits for them, and re-layouts: 3.05 us -> 1.31 us
    pallas_call x1, Pallas kernels: 28.2 us -> 27.4 us  [shards(): pl.pallas_call(functools.partial(kernel, n), out_shape=(pltpu.VMEM((1, ro...]
where the time goes in v3:
time: 29.5 us; the launch traced here: 29.4 us
  Pallas kernels  27.4 us (93%)
  local copies, waits for them, and re-layouts  1.31 us (4%)
  between operations  0.64 us (2%)
    pallas_call x1, Pallas kernels, shards(): pl.pallas_call(functools.partial(kernel, n), out_shape=(pltpu.VMEM((1, ro...  27.4 us
    unnamed x2, local copies, waits for them, and re-layouts  1.31 us

profile of v3, /device:TPU:0, one launch (start us, length us, event | category | flops | bytes accessed | tf_op | source)
XLA Modules:
  0.0 29.4 jit_solution(14765445915596143997)
XLA Ops:
  0.6 27.4 %shard_map.104 = (f32[1,128]{1,0:T(1,128)S(1)}, bf16[128,2048]{1,0:T(8,128)(2,1)S(1)}) custom-call(bf16[128,2048]{1,0:T(8,128)(2,1)} %llama.1, bf16[128,2432]{1,0:T(8,128)(2,1)} %qwen.1, bf16[128,4096]{1,0:T(8,128)(2,1)} %gemma.1, bf16[128,2048]{1,0:T(8,128)(2,1)} %student.1, s32[3,32]{1,0:T(4,128)} %bitcast.6, s32[3,38]{1,0:T(4,128)} %bitcast.7, ...), custom_call_target="tpu_custom_call" | custom-call | tf_op jit(solution)/shard_map/pallas_call | solution.py:316
  28.1 0.5 %copy.13 = f32[128]{0:T(128)} copy(f32[128]{0:T(128)S(1)} %bitcast.5) | data formatting | bytes 1024
  28.6 0.8 %copy.14 = bf16[128,2048]{1,0:T(8,128)(2,1)} copy(bf16[128,2048]{1,0:T(8,128)(2,1)S(1)} %get-tuple-element.7) | data formatting | bytes 1048576
